TPU v7x, 32 devices: a whole 2x2x4 slice. The times are simulated.
32 devices in a mesh: seq: 4 (over y, x), blk: 8 (over z, core).
Axes of the slice: x: 2, y: 2, z: 4, core: 2. Of those that a mesh axis runs over, the one named last changes fastest.
Arguments:
- activations: bfloat16 [2, 16, 512, 4096], P(None, 'blk', 'seq'), may hold values from -120 to 120, as said below
- out_grads: bfloat16 [2, 16, 512, 4096], P(None, 'blk', 'seq'), may hold values from -120 to 120, as said below
- lengths: int32 [16], P('blk'), may hold values from 256 to 512
- input_proj: bfloat16 [2, 64, 4096], replicated, may hold values from -0.09375 to 0.09375
- output_proj: bfloat16 [2, 64, 4096], replicated, may hold values from -0.09375 to 0.09375
- stored_proj: float32 [2048, 2, 64, 64], P(('seq', 'blk')), may hold values from -6 to 6
Outputs:
- scores: float32 [16, 2048], P('blk', 'seq')
Inputs may be any that keep to these rules, and one draw needn't show every extreme that they name: `activations`: finite values. `out_grads`: finite values.
All inputs are finite; a program needn't handle non-finite values.
Results may differ from a plain program's by a relative error of at most 0.0003.
Values sent between devices are 32-bit elements; how exact they have to be, the bound alone decides.
A program may use at most 64 MiB of HBM per device.

v0:
```python
import math

import jax
import jax.numpy as jnp
from jax import lax
from jax.sharding import PartitionSpec as P

damping = 0.1


def damped_inverse(moment, token_count):
    moment_mean = jnp.transpose(moment, (1, 0, 2)) / token_count
    proj_rank = moment_mean.shape[-1]
    identity = jnp.eye(proj_rank, dtype=jnp.float32)
    trace_part = jnp.trace(moment_mean, axis1=1, axis2=2)
    damped = moment_mean + (damping * trace_part / proj_rank)[:, None, None] * identity
    factor_low = jnp.linalg.cholesky(damped)
    return jax.vmap(lambda lower: jax.scipy.linalg.cho_solve((lower, True), identity))(factor_low)


def shards(activations, out_grads, lengths, input_proj, output_proj, stored_proj):
    hp = lax.Precision.HIGHEST
    layers, roll_dev, seq_dev, model_width = activations.shape
    proj_rank = input_proj.shape[1]
    seq_index = lax.axis_index("seq")
    blk_count = lax.axis_size("blk")
    train_dev = stored_proj.shape[0]
    positions = seq_index * seq_dev + jnp.arange(seq_dev, dtype=jnp.int32)
    live_mask = (positions[None, :] < lengths[:, None]).astype(jnp.float32)
    projected_in = (
        jnp.einsum("lrsd,lkd->lrsk", activations, input_proj, preferred_element_type=jnp.float32)
        * live_mask[None, :, :, None]
    )
    projected_out = (
        jnp.einsum("lrsd,lkd->lrsk", out_grads, output_proj, preferred_element_type=jnp.float32)
        * live_mask[None, :, :, None]
    )
    moment_in = jnp.einsum("lrsk,lrsm->klm", projected_in, projected_in, precision=hp)
    moment_out = jnp.einsum("lrsk,lrsm->klm", projected_out, projected_out, precision=hp)
    grad_terms = jnp.einsum("lrsp,lrsq->prlq", projected_out, projected_in, precision=hp)
    moment_in, moment_out, token_count = lax.psum(
        (moment_in, moment_out, jnp.sum(live_mask)), ("seq", "blk")
    )
    grad_rows = lax.psum_scatter(grad_terms, "seq", scatter_dimension=0, tiled=True)
    factor_in = damped_inverse(moment_in, token_count)
    factor_out = damped_inverse(moment_out, token_count)
    right_done = jnp.einsum("prlq,lqk->prlk", grad_rows, factor_in, precision=hp)
    precond = jnp.zeros((proj_rank, roll_dev, layers, proj_rank), jnp.float32) + jnp.einsum(
        "lap,prlk->arlk",
        factor_out,
        lax.all_gather(right_done, "seq", axis=0, tiled=True),
        precision=hp,
    )
    norm_scale = 1.0 / math.sqrt(layers * proj_rank * proj_rank)
    empty_scores = jnp.zeros((roll_dev * blk_count, train_dev), jnp.float32)
    partial_scores = (
        jnp.einsum(
            "prlk,tlpk->rt",
            lax.all_gather(precond, "blk", axis=1, tiled=True),
            stored_proj,
            precision=hp,
        )
        * norm_scale
    )
    local_scores = lax.dynamic_update_slice_in_dim(empty_scores, partial_scores, jnp.int32(0), 0)
    return lax.all_to_all(local_scores, "blk", split_axis=0, concat_axis=1, tiled=True)


def solution(mesh):
    return jax.shard_map(
        shards,
        mesh=mesh,
        in_specs=(
            P(None, "blk", "seq", None),
            P(None, "blk", "seq", None),
            P("blk"),
            P(),
            P(),
            P(("seq", "blk"), None, None, None),
        ),
        out_specs=P("blk", "seq"),
        check_vma=False,
    )
```

profile of v0, /device:TPU:0, one launch (start us, length us, event | category | flops | bytes accessed | tf_op | source)
XLA Modules:
  0.0 163.9 jit_solution(15823054299538239489)
XLA Ops:
  6.5 0.0 copy-start
  6.5 0.0 copy-start.2
  6.5 0.0 all-reduce.5.cloned.1.call-start
  6.5 0.0 copy-start.1
  6.6 0.9 compare_convert_fusion
  7.4 0.3 copy-done
  7.8 4.1 %convolution_multiply_fusion = f32[2,2,128,64]{2,3,1,0:T(8,128)S(1)} fusion(bf16[2,2,128,4096]{3,2,1,0:T(8,128)(2,1)} %param.10, bf16[2,64,4096]{2,1,0:T(8,128)(2,1)S(1)} %copy-done, f32[2,128]{1,0:T(2,128)S(1)} %compare_convert_fusion), kind=kOutput, calls=%fused_computation.2 | convolution fusion | flops 268468224 | bytes 5374976 | tf_op jit(solution)/shard_map/lrsd,lkd->lrsk/dot_general | solution.py:35
  11.9 0.0 copy-done.2
  11.9 0.0 copy-done.1
  11.9 0.0 copy-start.3
  12.0 1.4 convolution_multiply_fusion.1
  13.3 0.3 convolution_bitcast_fusion.1
  13.7 0.7 copy.25
  14.4 0.0 all-reduce.5.cloned.1.call-update
  14.5 0.3 convolution_bitcast_fusion.3
  14.7 0.3 convolution_bitcast_fusion.5
  15.0 0.0 copy-done.3
  15.0 0.7 fusion.19
  15.7 0.1 copy.21
  15.8 44.6 %all-reduce.6 = (f32[64,2,64]{0,2,1:T(8,128)S(1)}, f32[]{:T(128)}, f32[64,2,64]{0,2,1:T(8,128)S(1)}) all-reduce(f32[64,2,64]{0,2,1:T(8,128)S(1)} %convolution_bitcast_fusion.3, f32[]{:T(128)} %fusion.19, f32[64,2,64]{0,2,1:T(8,128)S(1)} %convolution_bitcast_fusion.5), channel_id=1, replica_groups=mesh['seq'=4,'blk'=8] {'seq','blk'}, use_global_device_ids=true, to_apply=%region_7.10 | all-reduce | flops 16385 | bytes 131080 | tf_op jit(solution)/shard_map/psum | solution.py:41
  60.4 0.8 fusion.9
  61.1 0.7 bitcast_add_fusion.1
  61.9 0.1 copy.20
  62.0 11.7 %custom-call.10 = f32[2,64,64]{2,1,0:T(8,128)S(1)} custom-call(f32[2,64,64]{2,1,0:T(8,128)S(1)} %fusion.13), custom_call_target="Cholesky" | custom-call | tf_op jit(solution)/shard_map/jit(cholesky)/cholesky | solution.py:17
  73.7 0.1 copy.28
  73.8 11.7 %custom-call.12 = f32[2,64,64]{2,1,0:T(8,128)S(1)} custom-call(f32[2,64,64]{2,1,0:T(8,128)S(1)} %fusion.8), custom_call_target="Cholesky" | custom-call | tf_op jit(solution)/shard_map/jit(cholesky)/cholesky | solution.py:17
  85.6 0.1 compare_reduce_fusion
  85.7 0.1 compare_reduce_fusion.1
  85.8 0.1 select_bitcast_fusion
  85.9 9.8 %custom-call.13 = f32[2,1,64,64]{2,3,1,0:T(8,128)S(1)} custom-call(f32[2,1,64,64]{3,2,1,0:T(8,128)S(1)} %get-tuple-element.16), custom_call_target="InvertDiagBlocksLowerTriangular" | custom-call | tf_op jit(solution)/shard_map/vmap(jit(_cho_solve))/triangular_solve | solution.py:18
  95.8 0.3 fusion.6
  96.1 0.2 convolution_bitcast_fusion.2
  96.3 9.8 %custom-call.11 = f32[2,1,64,64]{2,3,1,0:T(8,128)S(1)} custom-call(f32[2,1,64,64]{3,2,1,0:T(8,128)S(1)} %get-tuple-element.17), custom_call_target="InvertDiagBlocksLowerTriangular" | custom-call | tf_op jit(solution)/shard_map/vmap(jit(_cho_solve))/triangular_solve | solution.py:18
  106.1 0.3 fusion.11
  106.4 0.0 copy-start.4
  106.4 5.7 %copy.33 = f32[64,2,64,64]{2,0,1,3:T(8,128)} copy(f32[64,2,64,64]{3,2,1,0:T(8,128)} %param.14) | data formatting | bytes 4194304 | tf_op args[5]
  112.1 0.0 copy-done.4
  112.1 0.6 dynamic-slice
  113.4 0.2 convolution_bitcast_fusion.4
  113.6 0.0 all-reduce.5.cloned.1.call-done
  113.6 0.8 constant_dynamic-slice_fusion
  114.4 0.2 convolution_bitcast_fusion.6
  114.5 8.4 %all_gather.6 = f32[64,2,2,64]{3,0,2,1:T(8,128)S(1)} all-gather(f32[16,2,2,64]{3,0,2,1:T(8,128)S(1)} %copy.27), channel_id=1, replica_groups=mesh['seq'=4,'blk'=8] {'seq'}, dimensions={0}, use_global_device_ids=true | all-gather | bytes 81920 | tf_op jit(solution)/shard_map/all_gather | solution.py:51
  122.9 0.4 convolution_bitcast_fusion
  123.3 0.1 copy.31
  123.4 16.8 %all_gather.7 = f32[64,16,2,64]{3,0,2,1:T(8,128)S(1)} all-gather(f32[64,2,2,64]{3,0,2,1:T(8,128)S(1)} %copy.31), channel_id=1, replica_groups=mesh['seq'=4,'blk'=8] {'blk'}, dimensions={1}, use_global_device_ids=true | all-gather | bytes 589824 | tf_op jit(solution)/shard_map/all_gather | solution.py:59
  140.3 0.8 copy.32
  141.1 5.1 %fusion = f32[16,64]{1,0:T(8,128)S(1)} fusion(f32[64,16,2,64]{0,1,2,3:T(8,128)S(1)} %copy.32, f32[64,2,64,64]{2,0,1,3:T(8,128)} %copy.33), kind=kOutput, calls=%fused_computation.10 | convolution fusion | flops 100664320 | bytes 2625536 | tf_op jit(solution)/shard_map/prlk,tlpk->rt/dot_general | solution.py:57
  146.2 0.1 reshape.71
  146.3 8.8 %all_to_all.19 = f32[8,1,128]{2,1,0:T(1,128)S(1)} all-to-all(f32[8,1,128]{2,1,0:T(1,128)S(1)} %reshape.71), channel_id=1, replica_groups=mesh['seq'=4,'blk'=8] {'blk'}, dimensions={0} | all-to-all | bytes 8192 | tf_op jit(solution)/shard_map/all_to_all | solution.py:66
  155.1 0.5 broadcast.93
  155.6 0.7 reduce.4
  156.3 0.1 reshape.72
  156.4 0.7 all_to_all.17
  (11 shorter events, 0.1 us)
Async XLA Ops:
  6.5 1.2 copy-start
  6.5 5.4 %copy-start.2 = (bf16[2,64,4096]{2,1,0:T(8,128)(2,1)S(1)}, bf16[2,64,4096]{2,1,0:T(8,128)(2,1)}, u32[]{:S(2)}) copy-start(bf16[2,64,4096]{2,1,0:T(8,128)(2,1)} %param.12) | copy-start | bytes 3145732
  6.5 107.0 %all-reduce.5.cloned.1.call-start = ((), (), s32[]{:S(2)}) async-start(), calls=%async_computation.1 | async-start | bytes 262144
  6.5 5.4 %copy-start.1 = (bf16[2,2,128,4096]{3,2,1,0:T(8,128)(2,1)S(1)}, bf16[2,2,128,4096]{3,2,1,0:T(8,128)(2,1)}, u32[]{:S(2)}) copy-start(bf16[2,2,128,4096]{3,2,1,0:T(8,128)(2,1)} %param.9) | copy-start | bytes 12582916
  11.9 3.0 %copy-start.3 = (s32[2]{0:T(128)S(1)}, s32[2]{0:T(128)}, u32[]{:S(2)}) copy-start(s32[2]{0:T(128)} %param.11) | copy-start | bytes 28
  106.4 5.7 %copy-start.4 = (u32[32]{0:T(128)S(1)}, u32[32]{0:T(128)}, u32[]{:S(2)}) copy-start(u32[32]{0:T(128)} %constant.65) | copy-start | bytes 388
Sparse Core Ops, SparseCore 0:
  14.6 44.7 all-reduce.4
where the time goes:
time: 164 us
  blocking collectives  78.6 us (48%)
  other arithmetic  47.3 us (29%)
  between operations  14.3 us (9%)
  matrix products  13 us (8%)
  local copies, waits for them, and re-layouts  10.7 us (7%)
    psum x1, blocking collectives, shards(): lax.psum((moment_in, moment_out, jnp.sum(live_mask)), ('seq', 'blk'))  44.6 us
    another operation x6, other arithmetic, damped_inverse(): factor_low = jnp.linalg.cholesky(damped)  23.7 us
    another operation x4, other arithmetic, damped_inverse(): jax.scipy.linalg.cho_solve((lower, True), identity)  19.8 us
    all_gather x1, blocking collectives, shards(): lax.all_gather(precond, 'blk', axis=1, tiled=True)  16.8 us
    all_to_all x1, blocking collectives, shards(): lax.all_to_all(local_scores, 'blk', split_axis=0, concat_axis=1, tiled=True)  8.84 us
    all_gather x1, blocking collectives, shards(): lax.all_gather(right_done, 'seq', axis=0, tiled=True)  8.37 us
    unnamed x15, local copies, waits for them, and re-layouts  7.55 us
    dot_general x1, matrix products, shards(): jnp.einsum('prlk,tlpk->rt', lax.all_gather(precond, 'blk', axis=1, tiled=...  5.08 us
  transfers between devices with their start and end apart: 1, of which 0 were waited for; matrix products, arithmetic and copies ran while one was open for 33% of the time, Pallas kernels for 0%

commit v1 on v0

v1 whole, which is shorter than its diff:
```python
import functools
import math

import jax
import jax.numpy as jnp
from jax import lax
from jax.experimental import pallas as pl
from jax.experimental.pallas import tpu as pltpu
from jax.sharding import PartitionSpec as P

damping = 0.1
MESH = pl.DeviceIdType.MESH
f32, bf16 = jnp.float32, jnp.bfloat16
NT = (((1,), (1,)), ((), ()))
NN = (((1,), (0,)), ((), ()))
TN = (((0,), (0,)), ((), ()))


def mm(a, b, dims):
    return lax.dot_general(a, b, dims, preferred_element_type=f32)


def split(x):
    high = x.astype(bf16)
    return high, (x - high.astype(f32)).astype(bf16)


def invert(a_ref, cols_ref, layers, rank, width):
    rows = layers * rank
    lane = lax.broadcasted_iota(jnp.int32, (rows, width), 1)
    side_base = jnp.where(lane >= rank, rank, 0)
    sub8 = lax.broadcasted_iota(jnp.int32, (rank, width), 0)
    lane_in = lax.broadcasted_iota(jnp.int32, (1, width), 1) % rank
    group = 8

    def block(kb, _):
        k0 = pl.multiple_of(kb * group, group)
        mats = [a_ref[l * rank : (l + 1) * rank, :] for l in range(layers)]
        panels = [
            [
                jnp.take_along_axis(mats[l], side_base[:rank] + (k0 + j), axis=1)
                for j in range(group)
            ]
            for l in range(layers)
        ]
        heads = [a_ref[pl.ds(pl.multiple_of(l * rank + k0, group), group), :] for l in range(layers)]
        for l in range(layers):
            for j in range(group):
                cols_ref[j, l * rank : (l + 1) * rank, :] = panels[l][j]
        pheads = [
            [cols_ref[j, pl.ds(pl.multiple_of(l * rank + k0, group), group), :] for j in range(group)]
            for l in range(layers)
        ]
        sub_g = lax.broadcasted_iota(jnp.int32, (group, width), 0)
        for l in range(layers):
            for j in range(group):
                unit_row = jnp.where(lane_in == k0 + j, 1.0, 0.0)
                recip = 1.0 / pheads[l][j][j : j + 1, :]
                row = (heads[l][j : j + 1, :] + unit_row) * recip
                col_h = pheads[l][j] - jnp.where(sub_g == j, 1.0, 0.0)
                col = panels[l][j] - jnp.where(sub8 == k0 + j, 1.0, 0.0)
                heads[l] = heads[l] - col_h * row
                mats[l] = mats[l] - col * row
                for jj in range(j + 1, group):
                    part = pheads[l][jj][j : j + 1, :] * recip
                    pheads[l][jj] = pheads[l][jj] - col_h * part
                    panels[l][jj] = panels[l][jj] - col * part
        for l in range(layers):
            a_ref[l * rank : (l + 1) * rank, :] = mats[l]
        return 0

    lax.fori_loop(0, rank // group, block, 0)


def kernel(
    nseq, nblk, layers, roll_dev, seq_dev, rank, train_dev,
    act_hbm, grad_hbm, len_ref, pin_hbm, pout_hbm, store_hbm,
    out_ref,
    act, grad, pin, pout, store, pay_m, pay_g, rec_m, rec_g, part_m, gat_m, all_m, all_g,
    a_ref, cols_ref, t_ref, c_ref, s_hi, s_lo, snd, rec_s,
    load_sem, send_sem, sem1, sem2, sem3, sem4,
):
    width = 2 * rank
    seq_me, blk_me = lax.axis_index("seq"), lax.axis_index("blk")
    rows = rec_g.shape[1]
    rollouts = nblk * roll_dev
    hp = lax.Precision.HIGHEST

    loads = {}

    def load(name, src, dst):
        cp = pltpu.make_async_copy(src, dst, load_sem.at[len(loads)])
        cp.start()
        loads[name] = cp

    for l in range(layers):
        load(("pi", l), pin_hbm.at[l], pin.at[l])
        load(("po", l), pout_hbm.at[l], pout.at[l])
        for r in range(roll_dev):
            load(("a", l, r), act_hbm.at[l, r], act.at[l, r])
            load(("g", l, r), grad_hbm.at[l, r], grad.at[l, r])
    load("s", store_hbm, store)

    barrier = pltpu.get_barrier_semaphore()
    seq_peers = [lax.rem(seq_me + o, nseq) for o in range(1, nseq)]
    blk_peers = [lax.rem(blk_me + o, nblk) for o in range(1, nblk)]
    for s in seq_peers:
        pl.semaphore_signal(barrier, inc=1, device_id=(s, blk_me), device_id_type=MESH)
    for b in blk_peers:
        pl.semaphore_signal(barrier, inc=1, device_id=(seq_me, b), device_id_type=MESH)

    tok = lax.broadcasted_iota(jnp.int32, (seq_dev, width), 0) + seq_me * seq_dev
    live = [jnp.where(tok < len_ref[r], 1.0, 0.0) for r in range(roll_dev)]
    grams = {}
    for l in range(layers):
        loads[("pi", l)].wait()
        loads[("po", l)].wait()
        for r in range(roll_dev):
            loads[("a", l, r)].wait()
            pr_in = mm(act[l, r], pin[l], NT)
            loads[("g", l, r)].wait()
            pr_out = mm(grad[l, r], pout[l], NT)
            both = jnp.concatenate([pr_in, pr_out], axis=1) * live[r]
            grams[l, r] = lax.dot_general(both, both, TN, precision=hp, preferred_element_type=f32)
    count = sum(jnp.sum(live[r], axis=0, keepdims=True) for r in range(roll_dev))
    count = jnp.broadcast_to(count, (8, width))
    per = rank // rows if rows < rank else 1
    for l in range(layers):
        total = sum(grams[l, r] for r in range(roll_dev))
        moment = jnp.concatenate([total[:rank, :rank], total[rank:, rank:]], axis=1)
        for i in range(rank // rows):
            pay_m[l * (rank // rows) + i, :rows, :] = moment[i * rows : (i + 1) * rows]
    for r in range(roll_dev):
        g = jnp.concatenate([grams[l, r][rank:, :rank] for l in range(layers)], axis=1)
        for i in range(rank // rows):
            pay_g[r * (rank // rows) + i] = g[i * rows : (i + 1) * rows]
    for s in range(nseq):
        pay_m[s, rows:, :] = count

    pl.semaphore_wait(barrier, nseq - 1 + nblk - 1)

    sends = [0]
    started = []

    def send(src, dst, sem, dev):
        cp = pltpu.make_async_remote_copy(
            src_ref=src, dst_ref=dst, send_sem=send_sem.at[sends[0]], recv_sem=sem,
            device_id=dev, device_id_type=MESH,
        )
        sends[0] += 1
        cp.start()
        started.append(cp)
        return cp

    one_m = [send(pay_m.at[s], rec_m.at[o], sem1.at[0, o], (s, blk_me)) for o, s in enumerate(seq_peers)]
    one_g = [send(pay_g.at[s], rec_g.at[o], sem1.at[1, o], (s, blk_me)) for o, s in enumerate(seq_peers)]

    loads["s"].wait()
    quarter = rank // 4

    def prep(first):
        def one(i, _):
            for u in range(4):
                a = first + i * 4 + u
                parts = [
                    store[pl.ds(l * rank + a, train_dev, stride=layers * rank), :] for l in range(layers)
                ]
                hi, lo = split(jnp.concatenate(parts, axis=1))
                at = pl.ds(pl.multiple_of(a * width, width), width)
                s_hi[:, at] = hi
                s_lo[:, at] = lo
            return 0

        lax.fori_loop(0, quarter // 4, one, 0)

    prep(0)
    for cp in one_m:
        cp.wait_recv()
    part_m[...] = pay_m[seq_me] + sum(rec_m[o] for o in range(nseq - 1))

    two_m = [send(part_m, gat_m.at[blk_me], sem2.at[0, o], (seq_me, b)) for o, b in enumerate(blk_peers)]
    for cp in one_g:
        cp.wait_recv()
    all_g[blk_me, seq_me] = pay_g[seq_me] + sum(rec_g[o] for o in range(nseq - 1))
    mine = all_g.at[blk_me, seq_me]
    two_g = [send(mine, mine, sem2.at[1, o], (seq_me, b)) for o, b in enumerate(blk_peers)]
    gat_m[blk_me] = part_m[...]
    prep(quarter)
    for cp in two_m:
        cp.wait_recv()
    whole_m = gat_m[0]
    for b in range(1, nblk):
        whole_m = whole_m + gat_m[b]
    all_m[seq_me] = whole_m[:rows]
    token_count = whole_m[rows : rows + 1, :]

    mine_m = all_m.at[seq_me]
    three_m = [send(mine_m, mine_m, sem3.at[0, o], (s, blk_me)) for o, s in enumerate(seq_peers)]
    for cp in two_g:
        cp.wait_recv()
    mine_g = all_g.at[:, seq_me]
    three_g = [send(mine_g, mine_g, sem3.at[1, o], (s, blk_me)) for o, s in enumerate(seq_peers)]
    prep(2 * quarter)
    prep(3 * quarter)
    for cp in three_m:
        cp.wait_recv()

    moments = all_m[...].reshape(layers * rank, width)
    row_id = lax.broadcasted_iota(jnp.int32, (rank, width), 0)
    lane_id = lax.broadcasted_iota(jnp.int32, (rank, width), 1)
    on_diag = row_id == lane_id % rank
    left = lane_id[:1] < rank
    scales = []
    for l in range(layers):
        m = moments[l * rank : (l + 1) * rank]
        diag = jnp.sum(jnp.where(on_diag, m, 0.0), axis=0, keepdims=True)
        tr_in = jnp.sum(jnp.where(left, diag, 0.0), axis=1, keepdims=True)
        tr_out = jnp.sum(jnp.where(left, 0.0, diag), axis=1, keepdims=True)
        scale = rank / jnp.where(left, tr_in, tr_out)
        scales.append(scale)
        a_ref[l * rank : (l + 1) * rank, :] = m * scale + jnp.where(on_diag, damping, 0.0)
    invert(a_ref, cols_ref, layers, rank, width)
    inverses = [
        a_ref[l * rank : (l + 1) * rank, :] * (scales[l] * token_count) for l in range(layers)
    ]
    zero = jnp.zeros((rank, rank), f32)
    right = jnp.concatenate(
        [
            jnp.concatenate([inverses[l][:, :rank] if c == l else zero for c in range(layers)], axis=1)
            for l in range(layers)
        ],
        axis=0,
    )
    right_h, right_l = split(right)
    left_f = jnp.concatenate([inverses[l][:, rank:] for l in range(layers)], axis=0)
    left_h, left_l = split(left_f)

    for cp in three_g:
        cp.wait_recv()

    def apply(b, _):
        g = all_g[b].reshape(roll_dev * rank, width)
        g_h, g_l = split(g)
        t = mm(g_h, right_h, NN) + mm(g_l, right_h, NN) + mm(g_h, right_l, NN)
        for r in range(roll_dev):
            t_h, t_l = split(t[r * rank : (r + 1) * rank])
            x = mm(left_h, t_h, NN) + mm(left_l, t_h, NN) + mm(left_h, t_l, NN)
            packed = jnp.where(lane_id < rank, x[:rank], x[rank:])
            c_ref[pl.ds(pl.multiple_of((b * roll_dev + r) * rank, rank), rank), :] = packed
        return 0

    if nblk <= 8:
        for b in range(nblk):
            apply(b, 0)
    else:
        lax.fori_loop(0, nblk, apply, 0)

    c2 = jnp.concatenate([c_ref[pl.ds(a, rollouts, stride=rank), :] for a in range(rank)], axis=1)
    c_h, c_l = split(c2)
    s_h = s_hi[...]
    sc = mm(c_h, s_h, NT) + mm(c_l, s_h, NT) + mm(c_h, s_lo[...], NT)
    sc = sc * (1.0 / math.sqrt(layers * rank * rank))
    sc = jnp.concatenate([sc, sc], axis=1)
    for b in range(nblk):
        snd[b] = sc[b * roll_dev : (b + 1) * roll_dev]
    four = [send(snd.at[b], rec_s.at[blk_me], sem4.at[o], (seq_me, b)) for o, b in enumerate(blk_peers)]
    rec_s[blk_me] = snd[blk_me]
    for cp in four:
        cp.wait_recv()
    per_tile = width // train_dev
    for i in range(nblk // per_tile):
        out_ref[:, i * width : (i + 1) * width] = jnp.where(
            left, rec_s[per_tile * i], rec_s[per_tile * i + 1]
        )
    for cp in started:
        cp.wait_send()


def shards(nseq, nblk, activations, out_grads, lengths, input_proj, output_proj, stored_proj):
    layers, roll_dev, seq_dev, model_width = activations.shape
    rank = input_proj.shape[1]
    train_dev = stored_proj.shape[0]
    width = 2 * rank
    rows = layers * rank // nseq
    rollouts = nblk * roll_dev
    assert layers == 2 and roll_dev == 2 and train_dev == rank
    any_spec = pl.BlockSpec(memory_space=pl.ANY)
    n_loads = layers * 2 + layers * roll_dev * 2 + 1
    n_sends = 4 * (nseq - 1) + 3 * (nblk - 1)
    stored = stored_proj.reshape(train_dev * layers * rank, rank)
    flops = 4 * layers * roll_dev * seq_dev * model_width * rank
    return pl.pallas_call(
        functools.partial(kernel, nseq, nblk, layers, roll_dev, seq_dev, rank, train_dev),
        out_shape=jax.ShapeDtypeStruct((roll_dev, nblk * train_dev), f32),
        in_specs=[
            any_spec, any_spec, pl.BlockSpec(memory_space=pltpu.SMEM), any_spec, any_spec, any_spec,
        ],
        out_specs=pl.BlockSpec(memory_space=pltpu.VMEM),
        scratch_shapes=[
            pltpu.VMEM(activations.shape, bf16),
            pltpu.VMEM(out_grads.shape, bf16),
            pltpu.VMEM(input_proj.shape, bf16),
            pltpu.VMEM(output_proj.shape, bf16),
            pltpu.VMEM(stored.shape, f32),
            pltpu.VMEM((nseq, rows + 8, width), f32),
            pltpu.VMEM((nseq, rows, width), f32),
            pltpu.VMEM((nseq - 1, rows + 8, width), f32),
            pltpu.VMEM((nseq - 1, rows, width), f32),
            pltpu.VMEM((rows + 8, width), f32),
            pltpu.VMEM((nblk, rows + 8, width), f32),
            pltpu.VMEM((nseq, rows, width), f32),
            pltpu.VMEM((nblk, nseq, rows, width), f32),
            pltpu.VMEM((layers * rank, width), f32),
            pltpu.VMEM((8, layers * rank, width), f32),
            pltpu.VMEM((8, width), f32),
            pltpu.VMEM((rollouts * rank, width), f32),
            pltpu.VMEM((train_dev, rank * width), bf16),
            pltpu.VMEM((train_dev, rank * width), bf16),
            pltpu.VMEM((nblk, roll_dev, width), f32),
            pltpu.VMEM((nblk, roll_dev, width), f32),
            pltpu.SemaphoreType.DMA((n_loads,)),
            pltpu.SemaphoreType.DMA((n_sends,)),
            pltpu.SemaphoreType.DMA((2, nseq - 1)),
            pltpu.SemaphoreType.DMA((2, nblk - 1)),
            pltpu.SemaphoreType.DMA((2, nseq - 1)),
            pltpu.SemaphoreType.DMA((nblk - 1,)),
        ],
        compiler_params=pltpu.CompilerParams(
            collective_id=0, has_side_effects=True, vmem_limit_bytes=48 * 1024 * 1024
        ),
        cost_estimate=pl.CostEstimate(flops=flops, bytes_accessed=14 << 20, transcendentals=0),
    )(activations, out_grads, lengths, input_proj, output_proj, stored)


def solution(mesh):
    return jax.shard_map(
        functools.partial(shards, mesh.shape["seq"], mesh.shape["blk"]),
        mesh=mesh,
        in_specs=(
            P(None, "blk", "seq", None),
            P(None, "blk", "seq", None),
            P("blk"),
            P(),
            P(),
            P(("seq", "blk"), None, None, None),
        ),
        out_specs=P("blk", "seq"),
        check_vma=False,
    )
```

time: 164 us -> 41.5 us (0.25)
  blocking collectives: 78.6 us -> 0 us
  other arithmetic: 47.3 us -> 0 us
  Pallas kernels: 0 us -> 37.6 us
  between operations: 14.3 us -> 0.01 us
  matrix products: 13 us -> 0 us
  local copies, waits for them, and re-layouts: 10.7 us -> 3.7 us
    psum x1 -> x0, blocking collectives: 44.6 us -> none  [shards(): lax.psum((moment_in, moment_out, jnp.sum(live_mask)), ('seq', 'blk'))]
    another operation x10 -> x0, other arithmetic: 43.5 us -> none  [the longest x6 23.7 us: damped_inverse(): factor_low = jnp.linalg.cholesky(damped)]
    pallas_call x0 -> x1, Pallas kernels: none -> 37.6 us  [shards(): pl.pallas_call(functools.partial(kernel, nseq, nblk, layers, roll_dev, se...]
    all_gather x2 -> x0, blocking collectives: 25.2 us -> none  [the longest x1 16.8 us: shards(): lax.all_gather(precond, 'blk', axis=1, tiled=True)]
    dot_general x8 -> x0, matrix products: 12 us -> none  [the longest x1 5.08 us: shards(): jnp.einsum('prlk,tlpk->rt', lax.all_gather(precond, 'blk', axis=1, tiled=...]
    all_to_all x1 -> x0, blocking collectives: 8.84 us -> none  [shards(): lax.all_to_all(local_scores, 'blk', split_axis=0, concat_axis=1, tiled=True)]
    unnamed x15 -> x7, local copies, waits for them, and re-layouts: 7.55 us -> 3.7 us
  transfers between devices with their start and end apart: 1 -> 0, of which waited for: 0 -> 0; matrix products, arithmetic and copies ran while one was open for 33% -> 0% of each run, Pallas kernels for 0% -> 0%
where the time goes in v1:
time: 41.5 us; the launch traced here: 41.3 us
  Pallas kernels  37.6 us (91%)
  local copies, waits for them, and re-layouts  3.7 us (9%)
    pallas_call x1, Pallas kernels, shards(): pl.pallas_call(functools.partial(kernel, nseq, nblk, layers, roll_dev, se...  37.6 us
    unnamed x7, local copies, waits for them, and re-layouts  3.7 us

profile of v1, /device:TPU:0, one launch (start us, length us, event | category | flops | bytes accessed | tf_op | source)
XLA Modules:
  0.0 41.3 jit_solution(6182659787159394864)
XLA Ops:
  0.0 0.0 copy-start
  0.0 1.2 %copy-done = bf16[2,64,4096]{2,1,0:T(8,128)(2,1)S(1)} copy-done((bf16[2,64,4096]{2,1,0:T(8,128)(2,1)S(1)}, bf16[2,64,4096]{2,1,0:T(8,128)(2,1)}, u32[]{:S(2)}) %copy-start) | copy-done | bytes 1048600
  1.2 0.0 copy-start.1
  1.2 1.2 %copy-done.1 = bf16[2,64,4096]{2,1,0:T(8,128)(2,1)S(1)} copy-done((bf16[2,64,4096]{2,1,0:T(8,128)(2,1)S(1)}, bf16[2,64,4096]{2,1,0:T(8,128)(2,1)}, u32[]{:S(2)}) %copy-start.1) | copy-done | bytes 1048600
  2.5 0.0 copy-start.2
  2.5 0.7 %copy-done.2 = s32[2]{0:T(128)S(1)} copy-done((s32[2]{0:T(128)S(1)}, s32[2]{0:T(128)}, u32[]{:S(2)}) %copy-start.2) | copy-done | bytes 32
  3.1 37.6 %shard_map.64 = f32[2,512]{1,0:T(2,128)S(1)} custom-call(bf16[2,2,128,4096]{3,2,1,0:T(8,128)(2,1)} %act_hbm.1, bf16[2,2,128,4096]{3,2,1,0:T(8,128)(2,1)} %grad_hbm.1, s32[2]{0:T(128)S(1)} %copy-done.2, bf16[2,64,4096]{2,1,0:T(8,128)(2,1)S(1)} %copy-done, bf16[2,64,4096]{2,1,0:T(8,128)(2,1)S(1)} %copy-done.1, f32[8192,64]{1,0:T(8,128)} %bitcast.1), custom_call_target="tpu_custom_call" | custom-call | flops 536870912 | bytes 14680064 | tf_op jit(solution)/shard_map/pallas_call | solution.py:292
  40.7 0.6 %copy.8 = f32[2,512]{1,0:T(2,128)} copy(f32[2,512]{1,0:T(2,128)S(1)} %shard_map.64) | data formatting | bytes 8192
Async XLA Ops:
  0.0 1.2 %copy-start = (bf16[2,64,4096]{2,1,0:T(8,128)(2,1)S(1)}, bf16[2,64,4096]{2,1,0:T(8,128)(2,1)}, u32[]{:S(2)}) copy-start(bf16[2,64,4096]{2,1,0:T(8,128)(2,1)} %pin_hbm.1) | copy-start | bytes 3145732
  1.2 1.2 %copy-start.1 = (bf16[2,64,4096]{2,1,0:T(8,128)(2,1)S(1)}, bf16[2,64,4096]{2,1,0:T(8,128)(2,1)}, u32[]{:S(2)}) copy-start(bf16[2,64,4096]{2,1,0:T(8,128)(2,1)} %pout_hbm.1) | copy-start | bytes 3145732
  2.5 0.7 %copy-start.2 = (s32[2]{0:T(128)S(1)}, s32[2]{0:T(128)}, u32[]{:S(2)}) copy-start(s32[2]{0:T(128)} %len_ref.1) | copy-start | bytes 28

commit v2 on v1

--- a/solution.py
+++ b/solution.py
@@ -83,6 +83,10 @@
     width = 2 * rank
     seq_me, blk_me = lax.axis_index("seq"), lax.axis_index("blk")
     rows = rec_g.shape[1]
+    nz, ng = nblk // 2, 2 * nseq
+    mrows = all_m.shape[1]
+    core, z_me = lax.rem(blk_me, 2), lax.div(blk_me, 2)
+    group_me = seq_me * 2 + core
     rollouts = nblk * roll_dev
     hp = lax.Precision.HIGHEST
 
@@ -103,11 +107,15 @@
 
     barrier = pltpu.get_barrier_semaphore()
     seq_peers = [lax.rem(seq_me + o, nseq) for o in range(1, nseq)]
-    blk_peers = [lax.rem(blk_me + o, nblk) for o in range(1, nblk)]
-    for s in seq_peers:
-        pl.semaphore_signal(barrier, inc=1, device_id=(s, blk_me), device_id_type=MESH)
-    for b in blk_peers:
-        pl.semaphore_signal(barrier, inc=1, device_id=(seq_me, b), device_id_type=MESH)
+    shares = [lax.rem(group_me + o, ng) for o in range(1, ng)]
+    group = [(lax.div(g, 2), z_me * 2 + lax.rem(g, 2)) for g in shares]
+    line = [(seq_me, lax.rem(z_me + o, nz) * 2 + core) for o in range(1, nz)]
+    owners = [
+        lax.rem(z_me + o, nz) * 2 + lax.rem(core + c, 2) for o in range(nz) for c in range(2) if o or c
+    ]
+    greet = group + [(seq_me, b) for b in owners[1:]]
+    for peer in greet:
+        pl.semaphore_signal(barrier, inc=1, device_id=peer, device_id_type=MESH)
 
     tok = lax.broadcasted_iota(jnp.int32, (seq_dev, width), 0) + seq_me * seq_dev
     live = [jnp.where(tok < len_ref[r], 1.0, 0.0) for r in range(roll_dev)]
@@ -124,20 +132,19 @@
             grams[l, r] = lax.dot_general(both, both, TN, precision=hp, preferred_element_type=f32)
     count = sum(jnp.sum(live[r], axis=0, keepdims=True) for r in range(roll_dev))
     count = jnp.broadcast_to(count, (8, width))
-    per = rank // rows if rows < rank else 1
     for l in range(layers):
         total = sum(grams[l, r] for r in range(roll_dev))
         moment = jnp.concatenate([total[:rank, :rank], total[rank:, rank:]], axis=1)
-        for i in range(rank // rows):
-            pay_m[l * (rank // rows) + i, :rows, :] = moment[i * rows : (i + 1) * rows]
+        for i in range(rank // mrows):
+            pay_m[l * (rank // mrows) + i, :mrows, :] = moment[i * mrows : (i + 1) * mrows]
     for r in range(roll_dev):
         g = jnp.concatenate([grams[l, r][rank:, :rank] for l in range(layers)], axis=1)
         for i in range(rank // rows):
             pay_g[r * (rank // rows) + i] = g[i * rows : (i + 1) * rows]
-    for s in range(nseq):
-        pay_m[s, rows:, :] = count
-
-    pl.semaphore_wait(barrier, nseq - 1 + nblk - 1)
+    for g in range(ng):
+        pay_m[g, mrows:, :] = count
+
+    pl.semaphore_wait(barrier, len(greet))
 
     sends = [0]
     started = []
@@ -152,7 +159,7 @@
         started.append(cp)
         return cp
 
-    one_m = [send(pay_m.at[s], rec_m.at[o], sem1.at[0, o], (s, blk_me)) for o, s in enumerate(seq_peers)]
+    one_m = [send(pay_m.at[g], rec_m.at[o], sem1.at[0, o], group[o]) for o, g in enumerate(shares)]
     one_g = [send(pay_g.at[s], rec_g.at[o], sem1.at[1, o], (s, blk_me)) for o, s in enumerate(seq_peers)]
 
     loads["s"].wait()
@@ -176,30 +183,30 @@
     prep(0)
     for cp in one_m:
         cp.wait_recv()
-    part_m[...] = pay_m[seq_me] + sum(rec_m[o] for o in range(nseq - 1))
-
-    two_m = [send(part_m, gat_m.at[blk_me], sem2.at[0, o], (seq_me, b)) for o, b in enumerate(blk_peers)]
+    part_m[...] = pay_m[group_me] + sum(rec_m[o] for o in range(ng - 1))
+
+    two_m = [send(part_m, gat_m.at[z_me], sem2.at[0, o], peer) for o, peer in enumerate(line)]
     for cp in one_g:
         cp.wait_recv()
-    all_g[blk_me, seq_me] = pay_g[seq_me] + sum(rec_g[o] for o in range(nseq - 1))
-    mine = all_g.at[blk_me, seq_me]
-    two_g = [send(mine, mine, sem2.at[1, o], (seq_me, b)) for o, b in enumerate(blk_peers)]
-    gat_m[blk_me] = part_m[...]
+    all_g[z_me, core, seq_me] = pay_g[seq_me] + sum(rec_g[o] for o in range(nseq - 1))
+    mine = all_g.at[z_me, core, seq_me]
+    two_g = [send(mine, mine, sem2.at[1, o], peer) for o, peer in enumerate(line)]
+    gat_m[z_me] = part_m[...]
     prep(quarter)
     for cp in two_m:
         cp.wait_recv()
     whole_m = gat_m[0]
-    for b in range(1, nblk):
-        whole_m = whole_m + gat_m[b]
-    all_m[seq_me] = whole_m[:rows]
-    token_count = whole_m[rows : rows + 1, :]
-
-    mine_m = all_m.at[seq_me]
-    three_m = [send(mine_m, mine_m, sem3.at[0, o], (s, blk_me)) for o, s in enumerate(seq_peers)]
+    for z in range(1, nz):
+        whole_m = whole_m + gat_m[z]
+    all_m[group_me] = whole_m[:mrows]
+    token_count = whole_m[mrows : mrows + 1, :]
+
+    mine_m = all_m.at[group_me]
+    three_m = [send(mine_m, mine_m, sem3.at[0, o], peer) for o, peer in enumerate(group)]
     for cp in two_g:
         cp.wait_recv()
-    mine_g = all_g.at[:, seq_me]
-    three_g = [send(mine_g, mine_g, sem3.at[1, o], (s, blk_me)) for o, s in enumerate(seq_peers)]
+    mine_g = all_g.at[:, core, seq_me]
+    three_g = [send(mine_g, mine_g, sem3.at[1, o], peer) for o, peer in enumerate(group)]
     prep(2 * quarter)
     prep(3 * quarter)
     for cp in three_m:
@@ -239,7 +246,7 @@
         cp.wait_recv()
 
     def apply(b, _):
-        g = all_g[b].reshape(roll_dev * rank, width)
+        g = all_g[b // 2, b % 2].reshape(roll_dev * rank, width)
         g_h, g_l = split(g)
         t = mm(g_h, right_h, NN) + mm(g_l, right_h, NN) + mm(g_h, right_l, NN)
         for r in range(roll_dev):
@@ -263,7 +270,7 @@
     sc = jnp.concatenate([sc, sc], axis=1)
     for b in range(nblk):
         snd[b] = sc[b * roll_dev : (b + 1) * roll_dev]
-    four = [send(snd.at[b], rec_s.at[blk_me], sem4.at[o], (seq_me, b)) for o, b in enumerate(blk_peers)]
+    four = [send(snd.at[b], rec_s.at[blk_me], sem4.at[o], (seq_me, b)) for o, b in enumerate(owners)]
     rec_s[blk_me] = snd[blk_me]
     for cp in four:
         cp.wait_recv()
@@ -286,7 +293,9 @@
     assert layers == 2 and roll_dev == 2 and train_dev == rank
     any_spec = pl.BlockSpec(memory_space=pl.ANY)
     n_loads = layers * 2 + layers * roll_dev * 2 + 1
-    n_sends = 4 * (nseq - 1) + 3 * (nblk - 1)
+    ng, nz = 2 * nseq, nblk // 2
+    mrows = layers * rank // ng
+    n_sends = 3 * (ng - 1) + (nseq - 1) + 2 * (nz - 1) + nblk - 1
     stored = stored_proj.reshape(train_dev * layers * rank, rank)
     flops = 4 * layers * roll_dev * seq_dev * model_width * rank
     return pl.pallas_call(
@@ -302,14 +311,14 @@
             pltpu.VMEM(input_proj.shape, bf16),
             pltpu.VMEM(output_proj.shape, bf16),
             pltpu.VMEM(stored.shape, f32),
-            pltpu.VMEM((nseq, rows + 8, width), f32),
+            pltpu.VMEM((ng, mrows + 8, width), f32),
             pltpu.VMEM((nseq, rows, width), f32),
-            pltpu.VMEM((nseq - 1, rows + 8, width), f32),
+            pltpu.VMEM((ng - 1, mrows + 8, width), f32),
             pltpu.VMEM((nseq - 1, rows, width), f32),
-            pltpu.VMEM((rows + 8, width), f32),
-            pltpu.VMEM((nblk, rows + 8, width), f32),
-            pltpu.VMEM((nseq, rows, width), f32),
-            pltpu.VMEM((nblk, nseq, rows, width), f32),
+            pltpu.VMEM((mrows + 8, width), f32),
+            pltpu.VMEM((nz, mrows + 8, width), f32),
+            pltpu.VMEM((ng, mrows, width), f32),
+            pltpu.VMEM((nz, 2, nseq, rows, width), f32),
             pltpu.VMEM((layers * rank, width), f32),
             pltpu.VMEM((8, layers * rank, width), f32),
             pltpu.VMEM((8, width), f32),
@@ -320,13 +329,13 @@
             pltpu.VMEM((nblk, roll_dev, width), f32),
             pltpu.SemaphoreType.DMA((n_loads,)),
             pltpu.SemaphoreType.DMA((n_sends,)),
-            pltpu.SemaphoreType.DMA((2, nseq - 1)),
-            pltpu.SemaphoreType.DMA((2, nblk - 1)),
-            pltpu.SemaphoreType.DMA((2, nseq - 1)),
+            pltpu.SemaphoreType.DMA((2, ng - 1)),
+            pltpu.SemaphoreType.DMA((2, nz - 1)),
+            pltpu.SemaphoreType.DMA((2, ng - 1)),
             pltpu.SemaphoreType.DMA((nblk - 1,)),
         ],
         compiler_params=pltpu.CompilerParams(
-            collective_id=0, has_side_effects=True, vmem_limit_bytes=48 * 1024 * 1024
+            collective_id=0, has_side_effects=True, vmem_limit_bytes=60 * 1024 * 1024
         ),
         cost_estimate=pl.CostEstimate(flops=flops, bytes_accessed=14 << 20, transcendentals=0),
     )(activations, out_grads, lengths, input_proj, output_proj, stored)

time: 41.5 us -> 37.8 us (0.911)
  local copies, waits for them, and re-layouts: 3.7 us -> 1.28 us
  Pallas kernels: 37.6 us -> 36.4 us
    unnamed x7 -> x1, local copies, waits for them, and re-layouts: 3.7 us -> 1.28 us
    pallas_call x1, Pallas kernels: 37.6 us -> 36.4 us  [shards(): pl.pallas_call(functools.partial(kernel, nseq, nblk, layers, roll_dev, se...]
where the time goes in v2:
time: 37.8 us; the launch traced here: 37.7 us
  Pallas kernels  36.4 us (96%)
  local copies, waits for them, and re-layouts  1.28 us (3%)
    pallas_call x1, Pallas kernels, shards(): pl.pallas_call(functools.partial(kernel, nseq, nblk, layers, roll_dev, se...  36.4 us
    unnamed x1, local copies, waits for them, and re-layouts  1.28 us

profile of v2, /device:TPU:0, one launch (start us, length us, event | category | flops | bytes accessed | tf_op | source)
XLA Modules:
  0.0 37.7 jit_solution(17868962228407008037)
XLA Ops:
  0.0 36.4 %shard_map.64 = f32[2,512]{1,0:T(2,128)} custom-call(bf16[2,2,128,4096]{3,2,1,0:T(8,128)(2,1)} %act_hbm.1, bf16[2,2,128,4096]{3,2,1,0:T(8,128)(2,1)} %grad_hbm.1, s32[2]{0:T(128)} %len_ref.1, bf16[2,64,4096]{2,1,0:T(8,128)(2,1)} %pin_hbm.1, bf16[2,64,4096]{2,1,0:T(8,128)(2,1)} %pout_hbm.1, f32[8192,64]{1,0:T(8,128)} %bitcast.1), custom_call_target="tpu_custom_call" | custom-call | flops 536870912 | bytes 14680064 | tf_op jit(solution)/shard_map/pallas_call | solution.py:301
  36.4 1.3 %copy.8 = f32[2,512]{1,0:T(2,128)} copy(f32[2,512]{1,0:T(2,128)} %shard_map.64) | data formatting | bytes 8192

commit v3 on v2

--- a/solution.py
+++ b/solution.py
@@ -99,9 +99,10 @@
 
     for l in range(layers):
         load(("pi", l), pin_hbm.at[l], pin.at[l])
+        for r in range(roll_dev):
+            load(("a", l, r), act_hbm.at[l, r], act.at[l, r])
         load(("po", l), pout_hbm.at[l], pout.at[l])
         for r in range(roll_dev):
-            load(("a", l, r), act_hbm.at[l, r], act.at[l, r])
             load(("g", l, r), grad_hbm.at[l, r], grad.at[l, r])
     load("s", store_hbm, store)
 
@@ -122,13 +123,17 @@
     grams = {}
     for l in range(layers):
         loads[("pi", l)].wait()
+        model_width = act.shape[3]
+        for r in range(roll_dev):
+            loads[("a", l, r)].wait()
+        pr_in = mm(act[l].reshape(roll_dev * seq_dev, model_width), pin[l], NT)
         loads[("po", l)].wait()
         for r in range(roll_dev):
-            loads[("a", l, r)].wait()
-            pr_in = mm(act[l, r], pin[l], NT)
             loads[("g", l, r)].wait()
-            pr_out = mm(grad[l, r], pout[l], NT)
-            both = jnp.concatenate([pr_in, pr_out], axis=1) * live[r]
+        pr_out = mm(grad[l].reshape(roll_dev * seq_dev, model_width), pout[l], NT)
+        pair = jnp.concatenate([pr_in, pr_out], axis=1)
+        for r in range(roll_dev):
+            both = pair[r * seq_dev : (r + 1) * seq_dev] * live[r]
             grams[l, r] = lax.dot_general(both, both, TN, precision=hp, preferred_element_type=f32)
     count = sum(jnp.sum(live[r], axis=0, keepdims=True) for r in range(roll_dev))
     count = jnp.broadcast_to(count, (8, width))

time: 37.8 us -> 36.9 us (0.976)
  Pallas kernels: 36.4 us -> 35.5 us
    pallas_call x1, Pallas kernels: 36.4 us -> 35.5 us  [shards(): pl.pallas_call(functools.partial(kernel, nseq, nblk, layers, roll_dev, se...]
where the time goes in v3:
time: 36.9 us; the launch traced here: 36.7 us
  Pallas kernels  35.5 us (96%)
  local copies, waits for them, and re-layouts  1.28 us (3%)
    pallas_call x1, Pallas kernels, shards(): pl.pallas_call(functools.partial(kernel, nseq, nblk, layers, roll_dev, se...  35.5 us
    unnamed x1, local copies, waits for them, and re-layouts  1.28 us

profile of v3, /device:TPU:0, one launch (start us, length us, event | category | flops | bytes accessed | tf_op | source)
XLA Modules:
  0.0 36.7 jit_solution(5577368563212184668)
XLA Ops:
  0.0 35.5 %shard_map.64 = f32[2,512]{1,0:T(2,128)} custom-call(bf16[2,2,128,4096]{3,2,1,0:T(8,128)(2,1)} %act_hbm.1, bf16[2,2,128,4096]{3,2,1,0:T(8,128)(2,1)} %grad_hbm.1, s32[2]{0:T(128)} %len_ref.1, bf16[2,64,4096]{2,1,0:T(8,128)(2,1)} %pin_hbm.1, bf16[2,64,4096]{2,1,0:T(8,128)(2,1)} %pout_hbm.1, f32[8192,64]{1,0:T(8,128)} %bitcast.1), custom_call_target="tpu_custom_call" | custom-call | flops 536870912 | bytes 14680064 | tf_op jit(solution)/shard_map/pallas_call | solution.py:306
  35.5 1.3 %copy.8 = f32[2,512]{1,0:T(2,128)} copy(f32[2,512]{1,0:T(2,128)} %shard_map.64) | data formatting | bytes 8192
